TPU v7x, 32 devices: a whole 2x2x4 slice. The times are simulated.
32 devices in a mesh: mem: 8 (over z, x), rep: 4 (over y, core).
Axes of the slice: x: 2, y: 2, z: 4, core: 2. Of those that a mesh axis runs over, the one named last changes fastest.
Arguments:
- states: bfloat16 [2048, 384], P('rep'), may hold values from -6 to 6
- batch_index: int32 [2, 2048], P(None, 'rep'), may hold values from 0 to 511
- obs_pick: int32 [2, 128], replicated, may hold values from 0 to 383
- norm_gain: float32 [384], replicated, may hold values from 0.5 to 1.5
- w_in: bfloat16 [384, 1024], replicated, may hold values from -0.3125 to 0.3125
- b_in: float32 [1024], replicated, may hold values from -0.5 to 0.5
- member_params: bfloat16 [8, 393216], P('mem', 'rep'), may hold values from -6 to 6
- observed: bfloat16 [2, 2048, 128], P(None, 'rep'), may hold values from -6 to 6
- perturbation: bfloat16 [8, 2, 2048, 128], P('mem', None, 'rep'), may hold values from -6 to 6
- inv_sigma: float32 [2, 2048, 128], P(None, 'rep'), may hold values from 0.5 to 4
Outputs:
- updated_params: bfloat16 [8, 393216], P('mem', 'rep')
Inputs may be any that keep to these rules, and one draw needn't show every extreme that they name: `batch_index`: row number of a start state inside the block of 512 given states that belongs to its block of 512 batch rows. `obs_pick`: observed feature numbers; a number may repeat.
All inputs are finite; a program needn't handle non-finite values.
Results may differ from a plain program's by a relative error of at most 0.0056.
Values may be sent and summed in bfloat16 or wider, within the bound.
A program may use at most 64 MiB of HBM per device.

v0:
```python
import jax
import jax.numpy as jnp
from jax import lax
from jax.sharding import PartitionSpec as P

EPS = 1e-06
DT = 0.5


def hidden_layer(state, norm_gain, w_in, b_in):
    normed = (
        state * lax.rsqrt(jnp.mean(state * state, axis=-1, keepdims=True) + EPS) * norm_gain
    ).astype(jnp.bfloat16)
    return jax.nn.gelu(jnp.dot(normed, w_in, preferred_element_type=jnp.float32) + b_in).astype(
        jnp.bfloat16
    )


def member_sums(pieces):
    weighted, misfit_w = pieces
    count = weighted.shape[0]
    gram_list = []
    innov_list = []
    for item_index in range(weighted.shape[1]):
        flat = weighted[:, item_index].reshape(count, -1).astype(jnp.float32)
        anomaly = (flat - jnp.mean(flat, axis=0)).astype(jnp.bfloat16)
        misfit_flat = misfit_w[:, item_index].reshape(count, -1)
        gram_list.append(
            lax.dot_general(
                anomaly, anomaly, (((1,), (1,)), ((), ())), preferred_element_type=jnp.float32
            )
        )
        innov_list.append(
            lax.dot_general(
                anomaly, misfit_flat, (((1,), (1,)), ((), ())), preferred_element_type=jnp.float32
            )
        )
    return (jnp.stack(gram_list, axis=0), jnp.stack(innov_list, axis=0))


def solve_columns(system, right_side):
    lower_factor = jnp.linalg.cholesky(system)
    halfway = lax.linalg.triangular_solve(lower_factor, right_side, left_side=True, lower=True)
    return lax.linalg.triangular_solve(
        lower_factor, halfway, left_side=True, lower=True, transpose_a=True
    )


def on_device(
    states,
    batch_index,
    obs_pick,
    norm_gain,
    w_in,
    b_in,
    member_params,
    observed,
    perturbation,
    inv_sigma,
):
    local_members = member_params.shape[0]
    width = w_in.shape[1]
    features = w_in.shape[0]
    step_count = batch_index.shape[0]
    picked = obs_pick.shape[1]
    whole_params = lax.all_gather(member_params, "rep", axis=1, tiled=True)
    weights = whole_params.reshape(local_members, width, features)
    step_scale = DT * width ** (-0.5)
    start_state = jnp.take(states, batch_index, axis=0).astype(jnp.float32)
    shared = hidden_layer(start_state, norm_gain, w_in, b_in)
    current = start_state[None] + step_scale * jnp.einsum(
        "kbh,jhs->jkbs", shared, weights, preferred_element_type=jnp.float32
    )
    layer = hidden_layer(current, norm_gain, w_in, b_in)
    current = current + step_scale * jnp.einsum(
        "jkbh,jhs->jkbs", layer, weights, preferred_element_type=jnp.float32
    )
    feature_ids = lax.broadcasted_iota(jnp.int32, (step_count, features, picked), 1)
    selector = (feature_ids == obs_pick[:, None, :]).astype(jnp.float32)
    predicted = jnp.einsum("jkbs,ksf->jkbf", current, selector, precision=lax.Precision.HIGHEST)
    weighted = (predicted * inv_sigma).astype(jnp.bfloat16)
    misfit_w = (
        observed.astype(jnp.float32) * inv_sigma
        + perturbation.astype(jnp.float32)
        - predicted * inv_sigma
    ).astype(jnp.bfloat16)
    misfit_local = jnp.sum(jnp.square(misfit_w.astype(jnp.float32)))
    gram_items, innov_items = member_sums(
        (
            lax.all_to_all(weighted, "mem", split_axis=2, concat_axis=0, tiled=True),
            lax.all_to_all(misfit_w, "mem", split_axis=2, concat_axis=0, tiled=True),
        )
    )
    gram_matrix = jnp.sum(gram_items, axis=0)
    innovation = jnp.sum(innov_items, axis=0)
    members = gram_matrix.shape[0]
    entries = members * step_count * batch_index.shape[1] * lax.axis_size("rep") * picked
    identity = jnp.eye(members, dtype=jnp.float32)
    gram_matrix, innovation, misfit_total = lax.psum(
        (gram_matrix, innovation, misfit_local), ("mem", "rep")
    )
    system = gram_matrix + (1.0 + misfit_total / entries) * (members - 1) * identity
    coefficients = solve_columns(system, innovation)
    param_block = lax.all_to_all(member_params, "mem", split_axis=1, concat_axis=0, tiled=True)
    params_f = param_block.astype(jnp.float32)
    spread = params_f - jnp.mean(params_f, axis=0)
    change = jnp.einsum("kj,kp->jp", coefficients, spread, precision=lax.Precision.HIGHEST)
    renewed = (params_f + change).astype(jnp.bfloat16)
    return lax.all_to_all(renewed, "mem", split_axis=0, concat_axis=1, tiled=True)


def solution(mesh):
    placed = (
        P("rep", None),
        P(None, "rep"),
        P(),
        P(),
        P(),
        P(),
        P("mem", "rep"),
        P(None, "rep", None),
        P("mem", None, "rep", None),
        P(None, "rep", None),
    )
    return jax.shard_map(
        on_device, mesh=mesh, in_specs=placed, out_specs=P("mem", "rep"), check_vma=False
    )
```

profile of v0, /device:TPU:0, one launch (start us, length us, event | category | flops | bytes accessed | tf_op | source)
XLA Modules:
  0.0 154.2 jit_solution(10128250611705401600)
XLA Ops:
  0.6 2.8 %reduce.16 = bf16[8,12288]{1,0:T(8,128)(2,1)S(1)} reduce(bf16[8,1,12288]{2,1,0:T(2,128)(2,1)} %bitcast.133, bf16[]{:T(256)} %broadcast.183), dimensions={1}, to_apply=%bitcast.110.reduce_sub_computation | reduce | bytes 393218
  3.4 0.8 reshape.213
  4.2 7.3 %all-to-all-start = ((bf16[8,2,6144]{2,1,0:T(2,128)(2,1)}), bf16[8,2,6144]{2,1,0:T(2,128)(2,1)}, u32[]{:S(2)}, u32[]{:S(2)}) async-start(bf16[8,2,6144]{2,1,0:T(2,128)(2,1)} %reshape.213), calls=%async_computation | async-start | bytes 393216 | tf_op jit(solution)/shard_map/all_to_all | solution.py:104
  11.5 0.7 fusion.74
  12.1 0.7 compare_and_fusion
  12.8 12.9 %all_gather.3 = bf16[1,393216]{1,0:T(2,128)(2,1)S(1)} all-gather(bf16[1,98304]{1,0:T(2,128)(2,1)S(1)} %copy-done.2), channel_id=1, replica_groups=mesh['mem'=8,'rep'=4] {'rep'}, dimensions={1}, use_global_device_ids=true | all-gather | bytes 983040 | tf_op jit(solution)/shard_map/all_gather | solution.py:66
  25.7 16.3 %reduce.14 = bf16[393216]{0:T(1024)(128)(2,1)S(1)} reduce(bf16[1,393216]{1,0:T(2,128)(2,1)S(1)} %all_gather.3, bf16[]{:T(256)} %constant.98), dimensions={0}, to_apply=%all_gather.3.reduce_sub_computation | reduce | bytes 1572866 | tf_op jit(solution)/shard_map/all_gather | solution.py:66
  42.1 1.2 reshape.185
  43.3 1.3 reshape.205
  44.6 4.1 %gather_fusion = bf16[1024,384]{1,0:T(8,128)(2,1)S(1)} fusion(bf16[512,384]{1,0:T(8,128)(2,1)S(1)} %copy-done.1, s32[1024]{0:T(1024)S(1)} %broadcast_clamp_fusion), kind=kCustom, calls=%fused_computation | custom fusion | bytes 1576960 | tf_op jit(solution)/shard_map/jit(_take)/gather | solution.py:69
  49.2 1.2 copy.50
  50.4 4.1 %multiply_reduce_fusion = (f32[2,512]{1,0:T(2,128)S(1)}, f32[1,2,512,384]{2,3,1,0:T(8,128)S(1)}) fusion(bf16[1024,384]{1,0:T(8,128)(2,1)} %reshape.185, f32[1024]{0:T(1024)S(1)} %copy-done.6, bf16[384,1024]{1,0:T(8,128)(2,1)S(1)} %copy-done, f32[384]{0:T(512)S(1)} %copy-done.7, f32[2,512]{1,0:T(2,128)S(1)} %add_rsqrt_fusion.1, ...), kind=kOutput, calls=%fused_computation.33 | convolution fusion | flops 1625422848 | bytes 4733440 | tf_op jit(solution)/shard_map/kbh,jhs->jkbs/dot_general | solution.py:71
  54.5 5.2 %fusion.27 = f32[2,512,384]{1,2,0:T(8,128)} fusion(bf16[1024,384,1]{1,0,2:T(8,128)(2,1)} %reshape.205, f32[1024]{0:T(1024)S(1)} %copy-done.6, f32[1,2,512,384]{2,3,1,0:T(8,128)S(1)} %get-tuple-element.16, bf16[384,1024]{1,0:T(8,128)(2,1)S(1)} %copy-done, f32[384]{0:T(512)S(1)} %copy-done.7, f32[2,512]{1,0:T(2,128)S(1)} %add_rsqrt_fusion), kind=kOutput, calls=%fused_computation.35 | convolution fusion | flops 1622278144 | bytes 4728320 | tf_op jit(solution)/shard_map/jkbh,jhs->jkbs/dot_general | solution.py:75
  59.8 1.3 copy.55
  61.1 0.8 copy.64
  61.9 0.8 copy.66
  62.8 3.1 %multiply_reduce_fusion.1 = (f32[]{:T(128)}, bf16[1,2,512,128]{2,3,1,0:T(8,128)(2,1)S(1)}, bf16[1,2,512,128]{2,3,1,0:T(8,128)(2,1)S(1)}) fusion(bf16[1,2,512,128]{2,3,1,0:T(8,128)(2,1)} %copy.66, f32[2,512,128]{1,2,0:T(8,128)S(1)} %copy.55, bf16[2,512,128]{1,2,0:T(8,128)(2,1)} %copy.64, f32[1,2,512,384]{2,3,1,0:T(8,128)S(1)} %get-tuple-element.16, ...), kind=kOutput, calls=%fused_computation.56 | convolution fusion | flops 606306304 | bytes 4719620 | tf_op jit(solution)/shard_map/jkbs,ksf->jkbf/dot_general | solution.py:80
  65.9 0.9 copy.56
  66.7 0.9 copy.72
  67.6 6.0 %all-to-all-start.1 = ((bf16[1,2,512,128]{3,1,0,2:T(2,128)(2,1)}), bf16[1,2,512,128]{3,1,0,2:T(2,128)(2,1)S(1)}, u32[]{:S(2)}, u32[]{:S(2)}) async-start(bf16[1,2,512,128]{3,1,0,2:T(2,128)(2,1)} %copy.56), calls=%async_computation.1 | async-start | bytes 524288 | tf_op jit(solution)/shard_map/all_to_all | solution.py:90
  73.6 1.6 %reshape.214 = bf16[8,1,12288]{2,1,0:T(2,128)(2,1)S(1)} reshape(bf16[8,2,6144]{2,1,0:T(2,128)(2,1)} %all-to-all-done) | data formatting | bytes 393216
  75.5 7.5 %all-to-all-done.1 = bf16[1,2,512,128]{3,1,0,2:T(2,128)(2,1)S(1)} async-done(((bf16[1,2,512,128]{3,1,0,2:T(2,128)(2,1)}), bf16[1,2,512,128]{3,1,0,2:T(2,128)(2,1)S(1)}, u32[]{:S(2)}, u32[]{:S(2)}) %all-to-all-start.1) | async-done | bytes 262176 | tf_op jit(solution)/shard_map/all_to_all | solution.py:90
  83.0 3.6 %all-to-all-start.2 = ((bf16[1,2,512,128]{3,1,0,2:T(2,128)(2,1)}), bf16[1,2,512,128]{3,1,0,2:T(2,128)(2,1)S(1)}, u32[]{:S(2)}, u32[]{:S(2)}) async-start(bf16[1,2,512,128]{3,1,0,2:T(2,128)(2,1)} %copy.72), calls=%async_computation.2 | async-start | bytes 524288 | tf_op jit(solution)/shard_map/all_to_all | solution.py:91
  87.0 8.6 %all-to-all-done.2 = bf16[1,2,512,128]{3,1,0,2:T(2,128)(2,1)S(1)} async-done(((bf16[1,2,512,128]{3,1,0,2:T(2,128)(2,1)}), bf16[1,2,512,128]{3,1,0,2:T(2,128)(2,1)S(1)}, u32[]{:S(2)}, u32[]{:S(2)}) %all-to-all-start.2) | async-done | bytes 262176 | tf_op jit(solution)/shard_map/all_to_all | solution.py:91
  96.4 39.0 %all-reduce = (f32[8,8]{1,0:T(8,128)S(1)}, f32[8,8]{0,1:T(8,128)S(1)}, f32[]{:T(128)}) all-reduce(f32[8,8]{1,0:T(8,128)S(1)} %fusion.32, f32[8,8]{0,1:T(8,128)S(1)} %fusion.31, f32[]{:T(128)} %get-tuple-element.10), channel_id=1, replica_groups=mesh['mem'=8,'rep'=4] {'mem','rep'}, use_global_device_ids=true, to_apply=%region_9.10 | all-reduce | flops 129 | bytes 1032 | tf_op jit(solution)/shard_map/psum | solution.py:99
  136.2 0.7 cholesky.16
  137.1 0.6 compare_reduce_fusion
  137.7 0.6 select_select_fusion
  139.4 0.8 fusion.1
  140.3 0.8 reduce.17
  141.2 12.1 %all_to_all.65 = bf16[8,2,6144]{2,1,0:T(2,128)(2,1)S(1)} all-to-all(bf16[8,2,6144]{2,1,0:T(2,128)(2,1)S(1)} %reshape.215), channel_id=1, replica_groups=mesh['mem'=8,'rep'=4] {'mem'}, dimensions={0} | all-to-all | bytes 393216 | tf_op jit(solution)/shard_map/all_to_all | solution.py:109
  153.3 0.9 reshape.216
  (44 shorter events, 4.0 us)
Async XLA Ops:
  0.0 50.4 %copy-start = (bf16[384,1024]{1,0:T(8,128)(2,1)S(1)}, bf16[384,1024]{1,0:T(8,128)(2,1)}, u32[]{:S(2)}) copy-start(bf16[384,1024]{1,0:T(8,128)(2,1)} %param.14) | copy-start | bytes 2359300
  0.0 12.8 %copy-start.2 = (bf16[1,98304]{1,0:T(2,128)(2,1)S(1)}, bf16[1,98304]{1,0:T(2,128)(2,1)}, u32[]{:S(2)}) copy-start(bf16[1,98304]{1,0:T(2,128)(2,1)} %param.16) | copy-start | bytes 589828
  4.2 63.4 %all-to-all-start = ((bf16[8,2,6144]{2,1,0:T(2,128)(2,1)}), bf16[8,2,6144]{2,1,0:T(2,128)(2,1)}, u32[]{:S(2)}, u32[]{:S(2)}) async-start(bf16[8,2,6144]{2,1,0:T(2,128)(2,1)} %reshape.213), calls=%async_computation | async-start | bytes 393216 | tf_op jit(solution)/shard_map/all_to_all | solution.py:104
  42.1 2.5 %copy-start.1 = (bf16[512,384]{1,0:T(8,128)(2,1)S(1)}, bf16[512,384]{1,0:T(8,128)(2,1)}, u32[]{:S(2)}) copy-start(bf16[512,384]{1,0:T(8,128)(2,1)} %param.10) | copy-start | bytes 1179652
  48.7 1.7 %copy-start.6 = (f32[1024]{0:T(1024)S(1)}, f32[1024]{0:T(1024)}, u32[]{:S(2)}) copy-start(f32[1024]{0:T(1024)} %param.15) | copy-start | bytes 12292
  48.7 1.7 %copy-start.7 = (f32[384]{0:T(512)S(1)}, f32[384]{0:T(512)}, u32[]{:S(2)}) copy-start(f32[384]{0:T(512)} %param.13) | copy-start | bytes 4612
  54.5 6.5 %copy-start.3 = (bf16[2,512,128]{2,1,0:T(8,128)(2,1)S(1)}, bf16[2,512,128]{2,1,0:T(8,128)(2,1)}, u32[]{:S(2)}) copy-start(bf16[2,512,128]{2,1,0:T(8,128)(2,1)} %param.17) | copy-start | bytes 786436
  59.8 2.2 %copy-start.4 = (bf16[1,2,512,128]{3,2,1,0:T(8,128)(2,1)S(1)}, bf16[1,2,512,128]{3,2,1,0:T(8,128)(2,1)}, u32[]{:S(2)}) copy-start(bf16[1,2,512,128]{3,2,1,0:T(8,128)(2,1)} %param.18) | copy-start | bytes 786436
  59.8 3.0 %copy-start.5 = (s32[2,128]{1,0:T(2,128)S(1)}, s32[2,128]{1,0:T(2,128)}, u32[]{:S(2)}) copy-start(s32[2,128]{1,0:T(2,128)} %param.12) | copy-start | bytes 3076
  67.6 15.4 %all-to-all-start.1 = ((bf16[1,2,512,128]{3,1,0,2:T(2,128)(2,1)}), bf16[1,2,512,128]{3,1,0,2:T(2,128)(2,1)S(1)}, u32[]{:S(2)}, u32[]{:S(2)}) async-start(bf16[1,2,512,128]{3,1,0,2:T(2,128)(2,1)} %copy.56), calls=%async_computation.1 | async-start | bytes 524288 | tf_op jit(solution)/shard_map/all_to_all | solution.py:90
  83.0 12.6 %all-to-all-start.2 = ((bf16[1,2,512,128]{3,1,0,2:T(2,128)(2,1)}), bf16[1,2,512,128]{3,1,0,2:T(2,128)(2,1)S(1)}, u32[]{:S(2)}, u32[]{:S(2)}) async-start(bf16[1,2,512,128]{3,1,0,2:T(2,128)(2,1)} %copy.72), calls=%async_computation.2 | async-start | bytes 524288 | tf_op jit(solution)/shard_map/all_to_all | solution.py:91
where the time goes:
time: 155 us; the launch traced here: 154 us
  blocking collectives  64 us (41%)
  other arithmetic  25 us (16%)
  local copies, waits for them, and re-layouts  17 us (11%)
  starting transfers between devices  16.9 us (11%)
  waiting for transfers between devices  16.1 us (10%)
  matrix products  14.4 us (9%)
    psum x1, blocking collectives, on_device(): lax.psum((gram_matrix, innovation, misfit_local), ('mem', 'rep'))  39 us
    all_gather x1, other arithmetic, on_device(): whole_params = lax.all_gather(member_params, 'rep', axis=1, tiled=True)  16.3 us
    all_gather x1, blocking collectives, on_device(): whole_params = lax.all_gather(member_params, 'rep', axis=1, tiled=True)  12.9 us
    all_to_all x1, blocking collectives, on_device(): lax.all_to_all(renewed, 'mem', split_axis=0, concat_axis=1, tiled=True)  12.1 us
    all_to_all x1, waiting for transfers between devices, on_device(): lax.all_to_all(misfit_w, 'mem', split_axis=2, concat_axis=0, tiled=True)  8.61 us
    all_to_all x1, waiting for transfers between devices, on_device(): lax.all_to_all(weighted, 'mem', split_axis=2, concat_axis=0, tiled=True)  7.52 us
    all_to_all x1, starting transfers between devices, on_device(): lax.all_to_all(member_params, 'mem', split_axis=1, concat_axis=0, tiled=T...  7.25 us
    unnamed x25, local copies, waits for them, and re-layouts  7.04 us
  transfers between devices with their start and end apart: 3, of which 2 were waited for; matrix products, arithmetic and copies ran while one was open for 29% of the time, Pallas kernels for 0%

commit v1 on v0

--- a/solution.py
+++ b/solution.py
@@ -1,10 +1,402 @@
+import functools
+
 import jax
 import jax.numpy as jnp
 from jax import lax
+from jax.experimental import pallas as pl
+from jax.experimental.pallas import tpu as pltpu
 from jax.sharding import PartitionSpec as P
 
 EPS = 1e-06
 DT = 0.5
+F32 = jnp.float32
+BF16 = jnp.bfloat16
+MESH = pl.DeviceIdType.MESH
+
+
+def gelu(x):
+    return 0.5 * x * (1.0 + jnp.tanh(0.7978845608028654 * (x + 0.044715 * (x * x * x))))
+
+
+def dot(a, b):
+    return jnp.dot(a, b, preferred_element_type=F32)
+
+
+def halves(x):
+    high = x.astype(BF16)
+    low = (x - high.astype(F32)).astype(BF16)
+    return jnp.concatenate([high, low], axis=1)
+
+
+def kernel(
+    members,
+    entries,
+    states_ref,
+    index_ref,
+    pick_ref,
+    gain_ref,
+    w_in_ref,
+    b_in_ref,
+    params_ref,
+    observed_ref,
+    noise_ref,
+    sigma_ref,
+    out_ref,
+    w_buf,
+    p_buf,
+    e_send,
+    e_buf,
+    d_send,
+    d_buf,
+    g_send,
+    g_buf,
+    h_send,
+    h_buf,
+    new_buf,
+    hid,
+    w_sel,
+    state_acc,
+    pred_acc,
+    start_sel,
+    one_hot,
+    weight_sum,
+    anom,
+    anom_w,
+    resid,
+    pairs,
+    w_ssem,
+    w_rsem,
+    p_ssem,
+    p_rsem,
+    e_ssem,
+    e_rsem,
+    d_ssem,
+    d_rsem,
+    g_ssem,
+    g_rsem,
+    h_ssem,
+    h_rsem,
+    n_ssem,
+    n_rsem,
+):
+    m = lax.axis_index("mem")
+    r = lax.axis_index("rep")
+    planes = members // 2
+    z, x = m // 2, m % 2
+    reps = w_buf.shape[0]
+    rows, features = states_ref.shape
+    steps, _ = index_ref.shape
+    picked = pick_ref.shape[1]
+    chunk = rows // members
+    depth = params_ref.shape[0]
+    width = w_in_ref.shape[1]
+    block = depth // members
+    scale = DT * width ** (-0.5)
+
+    sibling = r + 1 - 2 * (r % 2)
+    across = (r + 2) % reps
+    diagonal = (sibling + 2) % reps
+
+    far_first = sorted(range(planes), key=lambda d: -min(d, planes - d))
+    steps_away = [(dz, dx) for dz in far_first for dx in range(2) if (dz, dx) != (0, 0)]
+
+    def partner(dz, dx):
+        return ((z + dz) % planes) * 2 + (x + dx) % 2
+
+    def source(dz, dx):
+        return ((z + planes - dz) % planes) * 2 + (x + 2 - dx) % 2
+
+    barrier = pltpu.get_barrier_semaphore()
+    for dz, dx in steps_away:
+        pl.semaphore_signal(barrier, inc=1, device_id=(partner(dz, dx), r), device_id_type=MESH)
+    for other in (sibling, across, diagonal):
+        pl.semaphore_signal(barrier, inc=1, device_id=(m, other), device_id_type=MESH)
+    pl.semaphore_wait(barrier, members - 1 + 3)
+
+    def remote(src, dst, ssem, rsem, device):
+        return pltpu.make_async_remote_copy(
+            src_ref=src, dst_ref=dst, send_sem=ssem, recv_sem=rsem, device_id=device, device_id_type=MESH
+        )
+
+    to_across = remote(params_ref, w_buf.at[r], w_ssem.at[0], w_rsem.at[0], (m, across))
+    to_sibling = remote(params_ref, w_buf.at[r], w_ssem.at[1], w_rsem.at[1], (m, sibling))
+    relay = remote(w_buf.at[across], w_buf.at[across], w_ssem.at[2], w_rsem.at[2], (m, sibling))
+    to_across.start()
+    to_sibling.start()
+
+    p_copies = []
+    for dz, dx in steps_away:
+        to, slot = partner(dz, dx), dz * 2 + dx
+        copy = remote(
+            params_ref.at[pl.ds(pl.multiple_of(to * block, block), block)],
+            p_buf.at[m],
+            p_ssem.at[slot],
+            p_rsem.at[slot],
+            (to, r),
+        )
+        copy.start()
+        p_copies.append(copy)
+
+    state_ids = lax.broadcasted_iota(jnp.int32, (rows, index_ref.shape[1]), 0)
+    feature_ids = lax.broadcasted_iota(jnp.int32, (features, picked), 0)
+    for k in range(steps):
+        cols = slice(k * picked, (k + 1) * picked)
+        hot = (state_ids == index_ref[k : k + 1, :]).astype(F32).astype(BF16)
+        one_hot[k] = hot
+        choose = (feature_ids == pick_ref[k : k + 1, :]).astype(F32).astype(BF16)
+        start_sel[:, cols] = dot(states_ref[...], choose)
+        sigma = sigma_ref[k]
+        both = dot(hot, halves(sigma * sigma))
+        total = both[:, :picked] + both[:, picked:]
+        weight_sum[k] = total
+        target = observed_ref[k].astype(F32) * sigma + noise_ref[k].astype(F32)
+        both = dot(hot, halves(sigma * target))
+        e_value = both[:, :picked] + both[:, picked:] - total * start_sel[:, cols]
+        e_send[:, k] = e_value.astype(BF16).reshape(members, chunk, picked)
+
+    e_copies = []
+    for dz, dx in steps_away:
+        to, slot = partner(dz, dx), dz * 2 + dx
+        copy = remote(e_send.at[to], e_buf.at[m], e_ssem.at[slot], e_rsem.at[slot], (to, r))
+        copy.start()
+        e_copies.append(copy)
+    e_buf[m] = e_send[m]
+
+    gain = gain_ref[...]
+
+    def normed(v):
+        return (v * lax.rsqrt(jnp.mean(v * v, axis=-1, keepdims=True) + EPS) * gain).astype(BF16)
+
+    first = normed(states_ref[...].astype(F32))
+    for c in range(reps):
+        cols = slice(c * depth, (c + 1) * depth)
+        hid[c] = gelu(dot(first, w_in_ref[:, cols]) + b_in_ref[:, cols]).astype(BF16)
+
+    choose = jnp.concatenate(
+        [(feature_ids == pick_ref[k : k + 1, :]).astype(F32).astype(BF16) for k in range(steps)], axis=1
+    )
+
+    def use_shard(owner, shard, opening):
+        layer = hid[owner]
+        chosen = dot(shard, choose).astype(BF16)
+        w_sel[owner] = chosen
+        if opening:
+            state_acc[...] = dot(layer, shard)
+            pred_acc[...] = dot(layer, chosen)
+        else:
+            state_acc[...] += dot(layer, shard)
+            pred_acc[...] += dot(layer, chosen)
+
+    use_shard(r, params_ref[...], True)
+    to_sibling.wait_recv()
+    use_shard(sibling, w_buf[sibling], False)
+    to_across.wait_recv()
+    relay.start()
+    use_shard(across, w_buf[across], False)
+    relay.wait_recv()
+    use_shard(diagonal, w_buf[diagonal], False)
+
+    d_copies = []
+    part = 2 * chunk
+    for dz in far_first:
+        plane = (z + dz) % planes
+        at = pl.ds(pl.multiple_of(plane * part, part), part)
+        current = states_ref[at, :].astype(F32) + scale * state_acc[at, :]
+        second = normed(current)
+        total = pred_acc[at, :]
+        for c in range(reps):
+            cols = slice(c * depth, (c + 1) * depth)
+            layer = gelu(dot(second, w_in_ref[:, cols]) + b_in_ref[:, cols]).astype(BF16)
+            total += dot(layer, w_sel[c])
+        delta = scale * total
+        pred_acc[at, :] = delta
+        for k in range(steps):
+            value = delta[:, k * picked : (k + 1) * picked].astype(BF16)
+            d_send[pl.ds(plane * 2, 2), k] = value.reshape(2, chunk, picked)
+        for dx in range(2):
+            if (dz, dx) != (0, 0):
+                to, slot = plane * 2 + (x + dx) % 2, dz * 2 + dx
+                copy = remote(d_send.at[to], d_buf.at[m], d_ssem.at[slot], d_rsem.at[slot], (to, r))
+                copy.start()
+                d_copies.append(copy)
+    d_buf[m] = d_send[m]
+
+    squares = jnp.zeros((index_ref.shape[1], picked), F32)
+    for k in range(steps):
+        cols = slice(k * picked, (k + 1) * picked)
+        both = lax.dot_general(
+            one_hot[k],
+            halves(start_sel[:, cols] + pred_acc[:, cols]),
+            (((0,), (0,)), ((), ())),
+            preferred_element_type=F32,
+        )
+        predicted = both[:, :picked] + both[:, picked:]
+        sigma = sigma_ref[k]
+        miss = observed_ref[k].astype(F32) * sigma + noise_ref[k].astype(F32) - predicted * sigma
+        squares += miss * miss
+    misfit_local = jnp.sum(jnp.sum(squares, axis=0, keepdims=True), axis=1, keepdims=True)
+
+    mine = pl.ds(pl.multiple_of(m * chunk, chunk), chunk)
+    d_weight = weight_sum[:, mine, :]
+
+    for copy in e_copies:
+        copy.wait_recv()
+    for copy in d_copies:
+        copy.wait_recv()
+
+    mean = d_buf[0].astype(F32)
+    for j in range(1, members):
+        mean += d_buf[j].astype(F32)
+    mean = mean * (1.0 / members)
+    for j in range(members):
+        value = d_buf[j].astype(F32)
+        anom[j] = value - mean
+        anom_w[j] = (value - mean) * d_weight
+        resid[j] = e_buf[j].astype(F32) - value * d_weight
+    slabs = steps * chunk // 8
+    for j in range(members):
+        left = anom[j].reshape(slabs, 8, picked)
+        for l in range(members):
+            right = anom_w[l].reshape(slabs, 8, picked)
+            pairs[pl.ds((l * members + j) * 8, 8), :] = jnp.sum(left * right, axis=0)
+            right = resid[l].reshape(slabs, 8, picked)
+            pairs[pl.ds(((members + l) * members + j) * 8, 8), :] = jnp.sum(left * right, axis=0)
+    count = 2 * members * members
+    sums = pairs[pl.ds(0, count, stride=8), :]
+    for s in range(1, 8):
+        sums += pairs[pl.ds(s, count, stride=8), :]
+    sums = jnp.sum(sums, axis=1, keepdims=True)
+    lanes = lax.broadcasted_iota(jnp.int32, (members, 128), 1)
+    packed = jnp.where(lanes == 2 * members, misfit_local, 0.0)
+    for l in range(2 * members):
+        packed = jnp.where(lanes == l, sums[l * members : (l + 1) * members, :], packed)
+    g_send[...] = packed
+    g_buf[m] = packed
+
+    g_copies = []
+    for dz, dx in steps_away:
+        to, slot = partner(dz, dx), dz * 2 + dx
+        copy = remote(g_send, g_buf.at[m], g_ssem.at[slot], g_rsem.at[slot], (to, r))
+        copy.start()
+        g_copies.append(copy)
+    for copy in g_copies:
+        copy.wait_recv()
+    total = g_buf[0]
+    for j in range(1, members):
+        total += g_buf[j]
+    h_send[...] = total
+    h_buf[r] = total
+    h_copies = []
+    for slot, other in enumerate((sibling, across, diagonal)):
+        copy = remote(h_send, h_buf.at[r], h_ssem.at[slot], h_rsem.at[slot], (m, other))
+        copy.start()
+        h_copies.append(copy)
+    for copy in h_copies:
+        copy.wait_recv()
+    total = h_buf[0]
+    for j in range(1, reps):
+        total += h_buf[j]
+
+    row_ids = lax.broadcasted_iota(jnp.int32, (members, 128), 0)
+    misfit = total[:, 2 * members : 2 * members + 1] * (1.0 / entries)
+    table = total + jnp.where(row_ids == lanes, (1.0 + misfit) * (members - 1), 0.0)
+    for j in range(members):
+        row = table[j : j + 1, :] / table[j : j + 1, j : j + 1]
+        table = jnp.where(row_ids == j, row, table - table[:, j : j + 1] * row)
+    centred = table - jnp.sum(table, axis=0, keepdims=True) * (1.0 / members)
+
+    for copy in p_copies:
+        copy.wait_recv()
+    p_buf[m] = params_ref[pl.ds(pl.multiple_of(m * block, block), block), :]
+    values = [p_buf[k].astype(F32) for k in range(members)]
+    for j in range(members):
+        change = values[0] * centred[0:1, members + j : members + j + 1]
+        for k in range(1, members):
+            change += values[k] * centred[k : k + 1, members + j : members + j + 1]
+        new_buf[j] = (values[j] + change).astype(BF16)
+    n_copies = []
+    here = pl.ds(pl.multiple_of(m * block, block), block)
+    for dz, dx in steps_away:
+        to, slot = partner(dz, dx), dz * 2 + dx
+        copy = remote(new_buf.at[to], out_ref.at[here], n_ssem.at[slot], n_rsem.at[slot], (to, r))
+        copy.start()
+        n_copies.append(copy)
+    out_ref[here, :] = new_buf[m]
+    for dz, dx in steps_away:
+        slot = dz * 2 + dx
+        came = source(dz, dx)
+        remote(
+            new_buf.at[came],
+            out_ref.at[pl.ds(pl.multiple_of(came * block, block), block)],
+            n_ssem.at[slot],
+            n_rsem.at[slot],
+            (came, r),
+        ).wait_recv()
+    for copy in [to_across, to_sibling, relay] + p_copies + e_copies + d_copies + g_copies + h_copies + n_copies:
+        copy.wait_send()
+
+
+def fused(members, reps, entries, *args):
+    states, batch_index, obs_pick, norm_gain, w_in, b_in, params, observed, noise, sigma = args
+    rows, features = states.shape
+    width = w_in.shape[1]
+    steps, picked = obs_pick.shape
+    depth = width // reps
+    chunk = rows // members
+    block = depth // members
+    piece = (members, steps, chunk, picked)
+    dma = pltpu.SemaphoreType.DMA
+    vmem = pl.BlockSpec(memory_space=pltpu.VMEM)
+    scratch = [
+        pltpu.VMEM((reps, depth, features), BF16),
+        pltpu.VMEM((members, block, features), BF16),
+        pltpu.VMEM(piece, BF16),
+        pltpu.VMEM(piece, BF16),
+        pltpu.VMEM(piece, BF16),
+        pltpu.VMEM(piece, BF16),
+        pltpu.VMEM((members, 128), F32),
+        pltpu.VMEM((members, members, 128), F32),
+        pltpu.VMEM((members, 128), F32),
+        pltpu.VMEM((reps, members, 128), F32),
+        pltpu.VMEM((members, block, features), BF16),
+        pltpu.VMEM((reps, rows, depth), BF16),
+        pltpu.VMEM((reps, depth, steps * picked), BF16),
+        pltpu.VMEM((rows, features), F32),
+        pltpu.VMEM((rows, steps * picked), F32),
+        pltpu.VMEM((rows, steps * picked), F32),
+        pltpu.VMEM((steps, rows, batch_index.shape[1]), BF16),
+        pltpu.VMEM((steps, rows, picked), F32),
+        pltpu.VMEM(piece, F32),
+        pltpu.VMEM(piece, F32),
+        pltpu.VMEM(piece, F32),
+        pltpu.VMEM((2 * members * members * 8, picked), F32),
+        dma((3,)),
+        dma((3,)),
+    ]
+    for count in (members, members, members, members, 3, members):
+        scratch += [dma((count,)), dma((count,))]
+    return pl.pallas_call(
+        functools.partial(kernel, members, entries),
+        out_shape=jax.ShapeDtypeStruct((depth, features), BF16),
+        in_specs=[vmem] * 10,
+        out_specs=vmem,
+        scratch_shapes=scratch,
+        compiler_params=pltpu.CompilerParams(
+            collective_id=0, has_side_effects=True, vmem_limit_bytes=48 * 1024 * 1024
+        ),
+        cost_estimate=pl.CostEstimate(flops=4 * 10**9, bytes_accessed=4 * 10**6, transcendentals=10**6),
+    )(
+        states,
+        batch_index,
+        obs_pick,
+        norm_gain.reshape(1, features),
+        w_in,
+        b_in.reshape(1, width),
+        params.reshape(depth, features),
+        observed,
+        noise.reshape(noise.shape[1:]),
+        sigma,
+    ).reshape(params.shape)
 
 
 def hidden_layer(state, norm_gain, w_in, b_in):
@@ -46,7 +438,7 @@
     )
 
 
-def on_device(
+def spread_out(
     states,
     batch_index,
     obs_pick,
@@ -109,6 +501,15 @@
     return lax.all_to_all(renewed, "mem", split_axis=0, concat_axis=1, tiled=True)
 
 
+def on_device(states, batch_index, obs_pick, norm_gain, w_in, b_in, member_params, observed, perturbation, inv_sigma):
+    args = (states, batch_index, obs_pick, norm_gain, w_in, b_in, member_params, observed, perturbation, inv_sigma)
+    members, reps = lax.axis_size("mem"), lax.axis_size("rep")
+    if members <= 8 and reps == 4 and member_params.shape[0] == 1:
+        entries = members * batch_index.size * reps * obs_pick.shape[1]
+        return fused(members, reps, entries, *args)
+    return spread_out(*args)
+
+
 def solution(mesh):
     placed = (
         P("rep", None),

time: 155 us -> 46.7 us (0.30)
  blocking collectives: 64 us -> 0 us
  Pallas kernels: 0 us -> 37.8 us
  other arithmetic: 25 us -> 2.08 us
  starting transfers between devices: 16.9 us -> 0 us
  waiting for transfers between devices: 16.1 us -> 0 us
  matrix products: 14.4 us -> 0 us
  local copies, waits for them, and re-layouts: 17 us -> 6.42 us
    psum x1 -> x0, blocking collectives: 39 us -> none  [on_device(): lax.psum((gram_matrix, innovation, misfit_local), ('mem', 'rep'))]
    pallas_call x0 -> x1, Pallas kernels: none -> 37.8 us  [fused(): pl.pallas_call(functools.partial(kernel, members, entries), out_shape=jax...]
    all_to_all x3 -> x0, starting transfers between devices: 16.9 us -> none  [the longest x1 7.25 us: on_device(): lax.all_to_all(member_params, 'mem', split_axis=1, concat_axis=0, tiled=T...]
    all_gather x1 -> x0, other arithmetic: 16.3 us -> none  [on_device(): whole_params = lax.all_gather(member_params, 'rep', axis=1, tiled=True)]
    all_to_all x3 -> x0, waiting for transfers between devices: 16.1 us -> none  [the longest x1 8.61 us: on_device(): lax.all_to_all(misfit_w, 'mem', split_axis=2, concat_axis=0, tiled=True)]
    dot_general x8 -> x0, matrix products: 14.1 us -> none  [the longest x1 5.24 us: on_device(): jnp.einsum('jkbh,jhs->jkbs', layer, weights, preferred_element_type=jnp.f...]
    all_gather x1 -> x0, blocking collectives: 12.9 us -> none  [on_device(): whole_params = lax.all_gather(member_params, 'rep', axis=1, tiled=True)]
    all_to_all x1 -> x0, blocking collectives: 12.1 us -> none  [on_device(): lax.all_to_all(renewed, 'mem', split_axis=0, concat_axis=1, tiled=True)]
  transfers between devices with their start and end apart: 3 -> 0, of which waited for: 2 -> 0; matrix products, arithmetic and copies ran while one was open for 29% -> 0% of each run, Pallas kernels for 0% -> 0%
where the time goes in v1:
time: 46.7 us; the launch traced here: 46.4 us
  Pallas kernels  37.8 us (81%)
  local copies, waits for them, and re-layouts  6.42 us (14%)
  other arithmetic  2.08 us (4%)
    pallas_call x1, Pallas kernels, fused(): pl.pallas_call(functools.partial(kernel, members, entries), out_shape=jax...  37.8 us
    unnamed x17, local copies, waits for them, and re-layouts  5.56 us
    unnamed x1, other arithmetic  2.08 us

profile of v1, /device:TPU:0, one launch (start us, length us, event | category | flops | bytes accessed | tf_op | source)
XLA Modules:
  0.0 46.4 jit_solution(13232238930741413842)
XLA Ops:
  0.0 0.0 copy-start
  0.0 0.8 %reshape.15.gain_ref = f32[1,384]{1,0:T(1,128)S(1)} reshape(f32[384]{0:T(512)} %param.13) | data formatting | bytes 3072 | tf_op jit(solution)/shard_map/reshape | solution.py:392
  0.8 2.1 %reduce = bf16[98304]{0:T(1024)(128)(2,1)S(1)} reduce(bf16[1,98304]{1,0:T(2,128)(2,1)} %param.16, bf16[]{:T(256)} %constant.2), dimensions={0}, to_apply=%param.16.reduce_sub_computation | reduce | bytes 393218 | tf_op args[6]
  2.8 0.0 copy-start.5
  2.9 0.0 copy-start.6
  2.9 0.0 copy-start.7
  2.9 0.1 reshape.17.params_ref
  3.0 0.0 copy-done
  3.0 0.5 %copy-done.5 = s32[2,512]{1,0:T(2,128)S(1)} copy-done((s32[2,512]{1,0:T(2,128)S(1)}, s32[2,512]{1,0:T(2,128)}, u32[]{:S(2)}) %copy-start.5) | copy-done | bytes 4120
  3.5 0.0 copy-done.6
  3.5 0.0 copy-done.7
  3.6 0.0 copy-start.1
  3.6 1.0 %copy-done.1 = f32[2,512,128]{2,1,0:T(8,128)S(1)} copy-done((f32[2,512,128]{2,1,0:T(8,128)S(1)}, f32[2,512,128]{2,1,0:T(8,128)}, u32[]{:S(2)}) %copy-start.1) | copy-done | bytes 524312
  4.6 0.0 copy-start.2
  4.6 1.0 %copy-done.2 = bf16[512,384]{1,0:T(8,128)(2,1)S(1)} copy-done((bf16[512,384]{1,0:T(8,128)(2,1)S(1)}, bf16[512,384]{1,0:T(8,128)(2,1)}, u32[]{:S(2)}) %copy-start.2) | copy-done | bytes 393240
  5.6 0.0 copy-start.3
  5.6 0.9 %copy-done.3 = bf16[2,512,128]{2,1,0:T(8,128)(2,1)S(1)} copy-done((bf16[2,512,128]{2,1,0:T(8,128)(2,1)S(1)}, bf16[2,512,128]{2,1,0:T(8,128)(2,1)}, u32[]{:S(2)}) %copy-start.3) | copy-done | bytes 262168
  6.5 0.0 copy-start.4
  6.5 0.9 %copy-done.4 = bf16[1,2,512,128]{3,2,1,0:T(8,128)(2,1)S(1)} copy-done((bf16[1,2,512,128]{3,2,1,0:T(8,128)(2,1)S(1)}, bf16[1,2,512,128]{3,2,1,0:T(8,128)(2,1)}, u32[]{:S(2)}) %copy-start.4) | copy-done | bytes 262168
  7.5 37.8 %shard_map.100 = bf16[256,384]{1,0:T(8,128)(2,1)S(1)} custom-call(bf16[512,384]{1,0:T(8,128)(2,1)S(1)} %copy-done.2, s32[2,512]{1,0:T(2,128)S(1)} %copy-done.5, s32[2,128]{1,0:T(2,128)S(1)} %copy-done.7, f32[1,384]{1,0:T(1,128)S(1)} %reshape.15.gain_ref, bf16[384,1024]{1,0:T(8,128)(2,1)S(1)} %copy-done, f32[1,1024]{1,0:T(1,128)S(1)} %bitcast.7, ...), custom_call_target="tpu_custom_call" | custom-call | flops 4000000000 | bytes 4000000 | tf_op jit(solution)/shard_map/pallas_call | solution.py:378
  45.3 1.0 %copy.11 = bf16[1,1,256,384]{3,1,2,0:T(2,128)(2,1)} copy(bf16[1,1,256,384]{3,2,1,0:T(8,128)(2,1)S(1)} %bitcast.5) | data formatting | bytes 393216
Async XLA Ops:
  0.0 3.0 %copy-start = (bf16[384,1024]{1,0:T(8,128)(2,1)S(1)}, bf16[384,1024]{1,0:T(8,128)(2,1)}, u32[]{:S(2)}) copy-start(bf16[384,1024]{1,0:T(8,128)(2,1)} %w_in_ref.1) | copy-start | bytes 2359300
  2.8 0.7 %copy-start.5 = (s32[2,512]{1,0:T(2,128)S(1)}, s32[2,512]{1,0:T(2,128)}, u32[]{:S(2)}) copy-start(s32[2,512]{1,0:T(2,128)} %index_ref.1) | copy-start | bytes 12292
  2.9 0.7 %copy-start.6 = (f32[1024]{0:T(1024)S(1)}, f32[1024]{0:T(1024)}, u32[]{:S(2)}) copy-start(f32[1024]{0:T(1024)} %param.15) | copy-start | bytes 12292
  2.9 0.7 %copy-start.7 = (s32[2,128]{1,0:T(2,128)S(1)}, s32[2,128]{1,0:T(2,128)}, u32[]{:S(2)}) copy-start(s32[2,128]{1,0:T(2,128)} %pick_ref.1) | copy-start | bytes 3076
  3.6 1.0 %copy-start.1 = (f32[2,512,128]{2,1,0:T(8,128)S(1)}, f32[2,512,128]{2,1,0:T(8,128)}, u32[]{:S(2)}) copy-start(f32[2,512,128]{2,1,0:T(8,128)} %sigma_ref.1) | copy-start | bytes 1572868
  4.6 1.0 %copy-start.2 = (bf16[512,384]{1,0:T(8,128)(2,1)S(1)}, bf16[512,384]{1,0:T(8,128)(2,1)}, u32[]{:S(2)}) copy-start(bf16[512,384]{1,0:T(8,128)(2,1)} %states_ref.1) | copy-start | bytes 1179652
  5.6 0.9 %copy-start.3 = (bf16[2,512,128]{2,1,0:T(8,128)(2,1)S(1)}, bf16[2,512,128]{2,1,0:T(8,128)(2,1)}, u32[]{:S(2)}) copy-start(bf16[2,512,128]{2,1,0:T(8,128)(2,1)} %observed_ref.1) | copy-start | bytes 786436
  6.5 0.9 %copy-start.4 = (bf16[1,2,512,128]{3,2,1,0:T(8,128)(2,1)S(1)}, bf16[1,2,512,128]{3,2,1,0:T(8,128)(2,1)}, u32[]{:S(2)}) copy-start(bf16[1,2,512,128]{3,2,1,0:T(8,128)(2,1)} %param.18) | copy-start | bytes 786436

commit v2 on v1

--- a/solution.py
+++ b/solution.py
@@ -31,16 +31,16 @@
 def kernel(
     members,
     entries,
-    states_ref,
-    index_ref,
-    pick_ref,
-    gain_ref,
-    w_in_ref,
-    b_in_ref,
-    params_ref,
-    observed_ref,
-    noise_ref,
-    sigma_ref,
+    states_hbm,
+    index_hbm,
+    pick_hbm,
+    gain_hbm,
+    w_in_hbm,
+    b_in_hbm,
+    params_hbm,
+    observed_hbm,
+    noise_hbm,
+    sigma_hbm,
     out_ref,
     w_buf,
     p_buf,
@@ -78,6 +78,18 @@
     h_rsem,
     n_ssem,
     n_rsem,
+    states_ref,
+    index_ref,
+    pick_ref,
+    gain_ref,
+    w_in_ref,
+    b_in_ref,
+    params_ref,
+    observed_ref,
+    noise_ref,
+    sigma_ref,
+    raw,
+    in_sem,
 ):
     m = lax.axis_index("mem")
     r = lax.axis_index("rep")
@@ -111,6 +123,24 @@
         pl.semaphore_signal(barrier, inc=1, device_id=(partner(dz, dx), r), device_id_type=MESH)
     for other in (sibling, across, diagonal):
         pl.semaphore_signal(barrier, inc=1, device_id=(m, other), device_id_type=MESH)
+
+    def load(slot, src, dst):
+        copy = pltpu.make_async_copy(src, dst, in_sem.at[slot])
+        copy.start()
+        return copy
+
+    get_params = load(6, params_hbm, raw)
+    get_index = load(1, index_hbm, index_ref)
+    get_pick = load(2, pick_hbm, pick_ref)
+    get_states = load(0, states_hbm, states_ref)
+    get_sigma = load(9, sigma_hbm, sigma_ref)
+    get_observed = load(7, observed_hbm, observed_ref)
+    get_noise = load(8, noise_hbm, noise_ref)
+    get_gain = load(3, gain_hbm, gain_ref)
+    get_b_in = load(5, b_in_hbm, b_in_ref)
+    get_w_in = load(4, w_in_hbm, w_in_ref)
+    get_params.wait()
+    params_ref[...] = raw[...].reshape(depth, features)
     pl.semaphore_wait(barrier, members - 1 + 3)
 
     def remote(src, dst, ssem, rsem, device):
@@ -136,6 +166,13 @@
         )
         copy.start()
         p_copies.append(copy)
+
+    get_index.wait()
+    get_pick.wait()
+    get_states.wait()
+    get_sigma.wait()
+    get_observed.wait()
+    get_noise.wait()
 
     state_ids = lax.broadcasted_iota(jnp.int32, (rows, index_ref.shape[1]), 0)
     feature_ids = lax.broadcasted_iota(jnp.int32, (features, picked), 0)
@@ -162,7 +199,10 @@
         e_copies.append(copy)
     e_buf[m] = e_send[m]
 
-    gain = gain_ref[...]
+    get_gain.wait()
+    get_b_in.wait()
+    get_w_in.wait()
+    gain = gain_ref[...].reshape(1, features)
 
     def normed(v):
         return (v * lax.rsqrt(jnp.mean(v * v, axis=-1, keepdims=True) + EPS) * gain).astype(BF16)
@@ -347,6 +387,7 @@
     piece = (members, steps, chunk, picked)
     dma = pltpu.SemaphoreType.DMA
     vmem = pl.BlockSpec(memory_space=pltpu.VMEM)
+    hbm = pl.BlockSpec(memory_space=pltpu.HBM)
     scratch = [
         pltpu.VMEM((reps, depth, features), BF16),
         pltpu.VMEM((members, block, features), BF16),
@@ -375,28 +416,33 @@
     ]
     for count in (members, members, members, members, 3, members):
         scratch += [dma((count,)), dma((count,))]
+    operands = (
+        states,
+        batch_index,
+        obs_pick,
+        norm_gain,
+        w_in,
+        b_in.reshape(1, width),
+        params.reshape(depth, 1, features),
+        observed,
+        noise.reshape(noise.shape[1:]),
+        sigma,
+    )
+    for place, operand in enumerate(operands):
+        shape = (depth, features) if place == 6 else operand.shape
+        scratch.append(pltpu.VMEM(shape, operand.dtype))
+    scratch += [pltpu.VMEM((depth, 1, features), BF16), dma((10,))]
     return pl.pallas_call(
         functools.partial(kernel, members, entries),
         out_shape=jax.ShapeDtypeStruct((depth, features), BF16),
-        in_specs=[vmem] * 10,
+        in_specs=[hbm] * 10,
         out_specs=vmem,
         scratch_shapes=scratch,
         compiler_params=pltpu.CompilerParams(
-            collective_id=0, has_side_effects=True, vmem_limit_bytes=48 * 1024 * 1024
+            collective_id=0, has_side_effects=True, vmem_limit_bytes=63 * 1024 * 1024
         ),
         cost_estimate=pl.CostEstimate(flops=4 * 10**9, bytes_accessed=4 * 10**6, transcendentals=10**6),
-    )(
-        states,
-        batch_index,
-        obs_pick,
-        norm_gain.reshape(1, features),
-        w_in,
-        b_in.reshape(1, width),
-        params.reshape(depth, features),
-        observed,
-        noise.reshape(noise.shape[1:]),
-        sigma,
-    ).reshape(params.shape)
+    )(*operands).reshape(params.shape)
 
 
 def hidden_layer(state, norm_gain, w_in, b_in):

time: 46.7 us -> 40.8 us (0.87)
  local copies, waits for them, and re-layouts: 6.42 us -> 1.98 us
  other arithmetic: 2.08 us -> 0 us
  Pallas kernels: 37.8 us -> 38.7 us
    unnamed x17 -> x1, local copies, waits for them, and re-layouts: 5.56 us -> 1.98 us
    unnamed x1 -> x0, other arithmetic: 2.08 us -> none
    reshape x2 -> x0, local copies, waits for them, and re-layouts: 0.85 us -> none  [the longest x1 0.76 us: fused(): norm_gain.reshape(1, features)]
    pallas_call x1, Pallas kernels: 37.8 us -> 38.7 us  [fused(): pl.pallas_call(functools.partial(kernel, members, entries), out_shape=jax...]
where the time goes in v2:
time: 40.8 us; the launch traced here: 40.6 us
  Pallas kernels  38.7 us (95%)
  local copies, waits for them, and re-layouts  1.98 us (5%)
    pallas_call x1, Pallas kernels, fused(): pl.pallas_call(functools.partial(kernel, members, entries), out_shape=jax...  38.7 us
    unnamed x1, local copies, waits for them, and re-layouts  1.98 us

profile of v2, /device:TPU:0, one launch (start us, length us, event | category | flops | bytes accessed | tf_op | source)
XLA Modules:
  0.0 40.6 jit_solution(10647373140027805831)
XLA Ops:
  0.0 38.7 %shard_map.100 = bf16[256,384]{1,0:T(8,128)(2,1)} custom-call(bf16[512,384]{1,0:T(8,128)(2,1)} %states_hbm.1, s32[2,512]{1,0:T(2,128)} %index_hbm.1, s32[2,128]{1,0:T(2,128)} %pick_hbm.1, f32[384]{0:T(512)} %gain_hbm.1, bf16[384,1024]{1,0:T(8,128)(2,1)} %w_in_hbm.1, f32[1,1024]{1,0:T(1,128)} %bitcast.9, bf16[256,1,384]{2,1,0:T(2,128)(2,1)} %bitcast.7, ...), custom_call_target="tpu_custom_call" | custom-call | flops 4000000000 | bytes 4000000 | tf_op jit(solution)/shard_map/pallas_call | solution.py:435
  38.7 2.0 %copy.11 = bf16[1,1,256,384]{3,1,2,0:T(2,128)(2,1)} copy(bf16[1,1,256,384]{3,2,1,0:T(8,128)(2,1)} %bitcast.6) | data formatting | bytes 393216
